TPU v7x, 256 devices: a whole 4x4x8 slice. The times are simulated.
256 devices in a mesh: gx: 8 (over y, z_lo), gy: 32 (over x, z_hi, core).
Axes of the slice: x: 4, y: 4, z: 8 (z_hi: 4, z_lo: 2; z = z_hi * 2 + z_lo), core: 2. Of those that a mesh axis runs over, the one named last changes fastest.
Arguments:
- images: bfloat16 [196608, 1152], P(('gx', 'gy'))
- captions: bfloat16 [196608, 1152], P(('gx', 'gy'))
- logit_scale: float32 [1], replicated, may hold values from 10 to 120
Outputs:
- losses: float32 [196608], P(('gx', 'gy'))
- grad_images: float32 [196608, 1152], P(('gx', 'gy'))
- grad_captions: float32 [196608, 1152], P(('gx', 'gy'))
All inputs are finite; a program needn't handle non-finite values.
Results may differ from a plain program's by a relative error of at most 0.0055.
The roundings to bfloat16 on the way count: a program that leaves them out, or rounds other values in their place, can miss the bound.
Values may be sent and summed in bfloat16 or wider, within the bound.
No kernel may reach another device: no remote copies, remote signals or barrier semaphores. Data moves between devices by JAX's collectives and lax.ppermute only.
A program may use at most 128 MiB of HBM per device.

v0:
```python
import jax
import jax.numpy as jnp
from jax import lax
from jax.sharding import PartitionSpec as P


def padded(value, sides, width):
    for axis, dim in sides:
        devices, length = (lax.axis_size(axis), value.shape[dim])
        up = [(i, (i + 1) % devices) for i in range(devices)]
        down = [(j, i) for i, j in up]
        last = lax.slice_in_dim(value, length - width, length, axis=dim)
        first = lax.slice_in_dim(value, 0, width, axis=dim)
        before = lax.ppermute(last, axis, up)
        after = lax.ppermute(first, axis, down)
        value = jnp.concatenate([before, value, after], axis=dim)
    return value


def widen_unit(values):
    widened = values.astype(jnp.float32)
    inverse = lax.rsqrt(jnp.sum(widened * widened, axis=-1, keepdims=True) + 1e-06)
    return (widened * inverse, inverse)


def log_total(values, along):
    peak = jnp.max(values, axis=along, keepdims=True)
    return jnp.squeeze(peak, along) + jnp.log(jnp.sum(jnp.exp(values - peak), axis=along))


def body(images, captions, logit_scale):
    height = images.shape[0]
    factor = logit_scale[0]
    img_unit, img_inverse = widen_unit(images)
    cap_unit, cap_inverse = widen_unit(captions)
    img_half = img_unit.astype(jnp.bfloat16)
    cap_half = cap_unit.astype(jnp.bfloat16)
    cap_window = padded(cap_half, ((("gx", "gy"), 0),), height)
    scores = factor * lax.dot_general(
        img_half, cap_window, (((1,), (1,)), ((), ())), preferred_element_type=jnp.float32
    )
    row_lse = log_total(scores, 1)
    col_peak = jnp.max(scores, axis=0)
    col_sum = jnp.sum(jnp.exp(scores - col_peak[None, :]), axis=0)
    send_peak = jnp.concatenate([col_peak[:height], col_peak[2 * height :]])
    send_sum = jnp.concatenate([col_sum[:height], col_sum[2 * height :]])
    peak_rim, sum_rim = (
        padded(send_peak, ((("gx", "gy"), 0),), height),
        padded(send_sum, ((("gx", "gy"), 0),), height),
    )
    peaks = jnp.stack([peak_rim[:height], col_peak[height : 2 * height], peak_rim[3 * height :]])
    totals = jnp.stack([sum_rim[:height], col_sum[height : 2 * height], sum_rim[3 * height :]])
    summit = jnp.max(peaks, axis=0)
    col_lse = summit + jnp.log(jnp.sum(totals * jnp.exp(peaks - summit[None, :]), axis=0))
    lse_window = padded(col_lse, ((("gx", "gy"), 0),), height)
    positive = jnp.diagonal(scores[:, height : 2 * height])
    losses = 0.5 * (row_lse - positive) + 0.5 * (col_lse - positive)
    row_index = lax.broadcasted_iota(jnp.int32, scores.shape, 0)
    col_index = lax.broadcasted_iota(jnp.int32, scores.shape, 1)
    target = (col_index == row_index + height).astype(jnp.float32)
    weights = (
        0.5 * jnp.exp(scores - row_lse[:, None])
        + 0.5 * jnp.exp(scores - lse_window[None, :])
        - target
    ).astype(jnp.bfloat16)
    img_grad = factor * jnp.dot(weights, cap_window, preferred_element_type=jnp.float32)
    pieces = factor * lax.dot_general(
        weights, img_half, (((0,), (0,)), ((), ())), preferred_element_type=jnp.float32
    )
    outgoing = jnp.concatenate([pieces[:height], pieces[2 * height :]], axis=0)
    grad_window = padded(outgoing, ((("gx", "gy"), 0),), height)
    cap_grad = grad_window[:height] + pieces[height : 2 * height] + grad_window[3 * height :]
    grad_images = img_inverse * (
        img_grad - img_unit * jnp.sum(img_unit * img_grad, axis=-1, keepdims=True)
    )
    grad_captions = cap_inverse * (
        cap_grad - cap_unit * jnp.sum(cap_unit * cap_grad, axis=-1, keepdims=True)
    )
    return (losses, grad_images, grad_captions)


def solution(mesh):
    return jax.shard_map(
        body,
        mesh=mesh,
        in_specs=(P(("gx", "gy"), None), P(("gx", "gy"), None), P()),
        out_specs=(P(("gx", "gy")), P(("gx", "gy"), None), P(("gx", "gy"), None)),
        check_vma=False,
    )
```

profile of v0, /device:TPU:56, one launch (start us, length us, event | category | flops | bytes accessed | tf_op | source)
XLA Modules:
  0.0 219.6 jit_solution(9811228039154272748)
XLA Ops:
  0.6 2.6 %copy.10 = bf16[768,1152]{0,1:T(8,128)(2,1)S(1)} copy(bf16[768,1152]{1,0:T(8,128)(2,1)} %param.4) | data formatting | bytes 3538944 | tf_op args[1]
  4.1 7.6 %collective-permute-start.1 = (bf16[768,1152]{0,1:T(8,128)(2,1)S(1)}, bf16[768,1152]{0,1:T(8,128)(2,1)S(1)}, u32[]{:S(2)}, u32[]{:S(2)}) collective-permute-start(bf16[768,1152]{0,1:T(8,128)(2,1)S(1)} %fusion.2), channel_id=1, source_target_pairs={{1,0},{2,1},{3,2},{4,3},{5,4},{6,5},{7,6},{8,7},{9,8},{10,9},{11,1... | collective-permute-start | bytes 5308424 | tf_op jit(solution)/shard_map/ppermute | solution.py:15
  12.7 35.8 %collective-permute-done.1 = bf16[768,1152]{0,1:T(8,128)(2,1)S(1)} collective-permute-done((bf16[768,1152]{0,1:T(8,128)(2,1)S(1)}, bf16[768,1152]{0,1:T(8,128)(2,1)S(1)}, u32[]{:S(2)}, u32[]{:S(2)}) %collective-permute-start.1) | collective-permute-done | bytes 1769504 | tf_op jit(solution)/shard_map/ppermute | solution.py:15
  48.6 8.3 %collective-permute-done = bf16[768,1152]{0,1:T(8,128)(2,1)S(1)} collective-permute-done((bf16[768,1152]{0,1:T(8,128)(2,1)S(1)}, bf16[768,1152]{0,1:T(8,128)(2,1)S(1)}, u32[]{:S(2)}, u32[]{:S(2)}) %collective-permute-start) | collective-permute-done | bytes 1769504 | tf_op jit(solution)/shard_map/ppermute | solution.py:14
  56.8 5.0 %fusion.21 = (f32[768]{0:T(1024)S(1)}, f32[2304]{0:T(1024)S(1)}, f32[768,2304]{1,0:T(8,128)S(1)}) fusion(bf16[768,1152]{0,1:T(8,128)(2,1)S(1)} %collective-permute-done.1, bf16[768,1152]{0,1:T(8,128)(2,1)S(1)} %fusion.2, bf16[768,1152]{0,1:T(8,128)(2,1)S(1)} %collective-permute-done, bf16[768,1152]{1,0:T(8,128)(2,1)S(1)} %copy-done.1, ...), kind=kOutput, calls=%fused_computation.44 | convolution fusion | flops 4100748288 | bytes 14171140 | tf_op jit(solution)/shard_map/dot_general | solution.py:39
  62.5 6.9 %collective-permute-start.3 = (f32[768]{0:T(1024)}, f32[768]{0:T(1024)}, u32[]{:S(2)}, u32[]{:S(2)}) collective-permute-start(f32[768]{0:T(1024)} %get-tuple-element.27), channel_id=1, source_target_pairs={{1,0},{2,1},{3,2},{4,3},{5,4},{6,5},{7,6},{8,7},{9,8},{10,9},{11,1... | collective-permute-start | bytes 9224 | tf_op jit(solution)/shard_map/ppermute | solution.py:15
  69.4 2.9 %exponential_reduce_fusion.1 = (f32[768]{0:T(1024)}, f32[2304]{0:T(1024)S(1)}) fusion(f32[768,2304]{1,0:T(8,128)S(1)} %get-tuple-element.28, f32[768]{0:T(1024)S(1)} %get-tuple-element.14, f32[2304]{0:T(1024)S(1)} %get-tuple-element.15), kind=kLoop, calls=%fused_computation.5 | loop fusion | flops 7074816 | bytes 7102464 | tf_op jit(solution)/shard_map/reduce_sum | solution.py:28
  72.9 1.6 slice.42
  75.1 6.9 %collective-permute-start.5 = (f32[768]{0:T(1024)}, f32[768]{0:T(1024)}, u32[]{:S(2)}, u32[]{:S(2)}) collective-permute-start(f32[768]{0:T(1024)} %get-tuple-element.24), channel_id=1, source_target_pairs={{1,0},{2,1},{3,2},{4,3},{5,4},{6,5},{7,6},{8,7},{9,8},{10,9},{11,1... | collective-permute-start | bytes 9224 | tf_op jit(solution)/shard_map/ppermute | solution.py:15
  81.9 14.4 %gather_fusion = f32[768]{0:T(1024)} fusion(f32[768,768]{1,0:T(8,128)} %slice.42, s32[768]{0:T(1024)S(1)} %or_reduce_fusion), kind=kCustom, calls=%fused_computation | custom fusion | bytes 12288 | tf_op jit(solution)/shard_map/jit(diagonal)/cond/branch_0_fun/gather | solution.py:56
  96.3 0.7 fusion.23
  99.8 0.7 fusion.17
  100.5 1.3 add_multiply_fusion
  102.3 0.8 collective-permute-done.7
  103.1 6.8 %collective-permute-done.6 = f32[768]{0:T(1024)S(1)} collective-permute-done((f32[768]{0:T(1024)S(1)}, f32[768]{0:T(1024)S(1)}, u32[]{:S(2)}, u32[]{:S(2)}) %collective-permute-start.6) | collective-permute-done | bytes 3104 | tf_op jit(solution)/shard_map/ppermute | solution.py:14
  110.0 9.3 %convolution_multiply_fusion = f32[2304,1152]{0,1:T(8,128)S(1)} fusion(f32[]{:T(128)} %bitcast.3, bf16[768,1152]{1,0:T(8,128)(2,1)S(1)} %copy-done.1, f32[768]{0:T(1024)S(1)} %add_rsqrt_fusion.1, f32[768,2304]{1,0:T(8,128)} %copy-done, s32[768]{0:T(1024)S(1)} %iota_add_fusion, f32[2304]{0:T(1024)S(1)} %pad_maximum_fusion.3, f32[768]{0:T(1024)S(1)} %get-tuple-element.17), kind=kOutput, calls=%fused_computation.1 | convolution fusion | flops 4096327680 | bytes 19482628 | tf_op jit(solution)/shard_map/dot_general | solution.py:67
  119.3 3.3 %fusion.22 = (f32[768,1152]{0,1:T(8,128)}, f32[768,1152]{0,1:T(8,128)}) fusion(f32[2304,1152]{0,1:T(8,128)S(1)} %convolution_multiply_fusion), kind=kLoop, calls=%fused_computation.45 | loop fusion | bytes 14155776 | tf_op jit(solution)/shard_map/slice | solution.py:70
  122.6 6.9 %collective-permute-start.9 = (f32[768,1152]{0,1:T(8,128)}, f32[768,1152]{0,1:T(8,128)}, u32[]{:S(2)}, u32[]{:S(2)}) collective-permute-start(f32[768,1152]{0,1:T(8,128)} %get-tuple-element.20), channel_id=1, source_target_pairs={{1,0},{2,1},{3,2},{4,3},{5,4},{6,5},{7,6},{8,7},{9,8},{10,9},{11,1... | collective-permute-start | bytes 10616840 | tf_op jit(solution)/shard_map/ppermute | solution.py:15
  129.5 13.0 %fusion.6 = (f32[768]{0:T(1024)S(1)}, f32[768,1152]{1,0:T(8,128)}) fusion(bf16[768,1152]{1,0:T(8,128)(2,1)S(1)} %copy-done.1, f32[768]{0:T(1024)S(1)} %add_rsqrt_fusion.1, bf16[768,1152]{0,1:T(8,128)(2,1)} %copy-done.4, bf16[768,1152]{0,1:T(8,128)(2,1)} %copy-done.2, bf16[768,1152]{0,1:T(8,128)(2,1)} %copy-done.5, f32[768,2304]{1,0:T(8,128)} %copy-done, ...), kind=kOutput, calls=%fused_computation.19 | convolution fusion | flops 4111367424 | bytes 17716228 | tf_op jit(solution)/shard_map/dot_general | solution.py:66
  142.5 4.5 %fusion.8 = f32[768,1152]{1,0:T(8,128)} fusion(f32[768,1152]{1,0:T(8,128)} %get-tuple-element.30, bf16[768,1152]{1,0:T(8,128)(2,1)S(1)} %copy-done.1, f32[768]{0:T(1024)S(1)} %get-tuple-element.29, f32[768]{0:T(1024)S(1)} %add_rsqrt_fusion.1), kind=kLoop, calls=%fused_computation.21 | loop fusion | flops 4423680 | bytes 8853504 | tf_op jit(solution)/shard_map/mul | solution.py:73
  146.9 60.0 %collective-permute-done.8 = f32[768,1152]{0,1:T(8,128)S(1)} collective-permute-done((f32[768,1152]{0,1:T(8,128)}, f32[768,1152]{0,1:T(8,128)S(1)}, u32[]{:S(2)}, u32[]{:S(2)}) %collective-permute-start.8) | collective-permute-done | bytes 3538976 | tf_op jit(solution)/shard_map/ppermute | solution.py:14
  206.9 2.9 %fusion.10 = f32[768]{0:T(1024)S(1)} fusion(bf16[768,1152]{0,1:T(8,128)(2,1)S(1)} %copy.10, f32[768]{0:T(1024)S(1)} %add_rsqrt_fusion, f32[768,1152]{0,1:T(8,128)} %collective-permute-done.9, f32[768,1152]{0,1:T(8,128)S(1)} %collective-permute-done.8, f32[2304,1152]{0,1:T(8,128)S(1)} %convolution_multiply_fusion), kind=kLoop, calls=%fused_computation.23 | loop fusion | flops 5307648 | bytes 12392448 | tf_op jit(solution)/shard_map/reduce_sum | solution.py:77
  209.8 4.7 %fusion.12 = f32[768,1152]{0,1:T(8,128)} fusion(bf16[768,1152]{0,1:T(8,128)(2,1)S(1)} %copy.10, f32[768]{0:T(1024)S(1)} %fusion.10, f32[768]{0:T(1024)S(1)} %add_rsqrt_fusion, f32[768,1152]{0,1:T(8,128)} %collective-permute-done.9, f32[768,1152]{0,1:T(8,128)S(1)} %collective-permute-done.8, f32[2304,1152]{0,1:T(8,128)S(1)} %convolution_multiply_fusion), kind=kLoop, calls=%fused_computation.25 | loop fusion | flops 6193152 | bytes 15931392 | tf_op jit(solution)/shard_map/mul | solution.py:76
  214.5 5.2 %copy.11 = f32[768,1152]{1,0:T(8,128)} copy(f32[768,1152]{0,1:T(8,128)} %fusion.12) | data formatting | bytes 7077888
  (39 shorter events, 6.3 us)
Async XLA Ops:
  3.3 9.0 %copy-start.1 = (bf16[768,1152]{1,0:T(8,128)(2,1)S(1)}, bf16[768,1152]{1,0:T(8,128)(2,1)}, u32[]{:S(2)}) copy-start(bf16[768,1152]{1,0:T(8,128)(2,1)} %param.3) | copy-start | bytes 5308420
  4.0 57.8 %copy-start.2 = (bf16[768,1152]{0,1:T(8,128)(2,1)}, bf16[768,1152]{0,1:T(8,128)(2,1)S(1)}, u32[]{:S(2)}) copy-start(bf16[768,1152]{0,1:T(8,128)(2,1)S(1)} %fusion.2) | copy-start | bytes 5308420
  4.1 44.5 %collective-permute-start.1 = (bf16[768,1152]{0,1:T(8,128)(2,1)S(1)}, bf16[768,1152]{0,1:T(8,128)(2,1)S(1)}, u32[]{:S(2)}, u32[]{:S(2)}) collective-permute-start(bf16[768,1152]{0,1:T(8,128)(2,1)S(1)} %fusion.2), channel_id=1, source_target_pairs={{1,0},{2,1},{3,2},{4,3},{5,4},{6,5},{7,6},{8,7},{9,8},{10,9},{11,1... | collective-permute-start | bytes 5308424 | tf_op jit(solution)/shard_map/ppermute | solution.py:15
  11.6 45.2 %collective-permute-start = (bf16[768,1152]{0,1:T(8,128)(2,1)S(1)}, bf16[768,1152]{0,1:T(8,128)(2,1)S(1)}, u32[]{:S(2)}, u32[]{:S(2)}) collective-permute-start(bf16[768,1152]{0,1:T(8,128)(2,1)S(1)} %fusion.2), channel_id=1, source_target_pairs={{0,1},{1,2},{2,3},{3,4},{4,5},{5,6},{6,7},{7,8},{8,9},{9,10},{10,1... | collective-permute-start | bytes 5308424 | tf_op jit(solution)/shard_map/ppermute | solution.py:14
  48.6 13.3 %copy-start.4 = (bf16[768,1152]{0,1:T(8,128)(2,1)}, bf16[768,1152]{0,1:T(8,128)(2,1)S(1)}, u32[]{:S(2)}) copy-start(bf16[768,1152]{0,1:T(8,128)(2,1)S(1)} %collective-permute-done.1) | copy-start | bytes 5308420
  56.8 5.0 %copy-start.5 = (bf16[768,1152]{0,1:T(8,128)(2,1)}, bf16[768,1152]{0,1:T(8,128)(2,1)S(1)}, u32[]{:S(2)}) copy-start(bf16[768,1152]{0,1:T(8,128)(2,1)S(1)} %collective-permute-done) | copy-start | bytes 5308420
  61.8 10.5 %copy-start.3 = (f32[2304]{0:T(1024)}, f32[2304]{0:T(1024)S(1)}, u32[]{:S(2)}) copy-start(f32[2304]{0:T(1024)S(1)} %get-tuple-element.15) | copy-start | bytes 27652
  61.8 11.1 %copy-start = (f32[768,2304]{1,0:T(8,128)}, f32[768,2304]{1,0:T(8,128)S(1)}, u32[]{:S(2)}) copy-start(f32[768,2304]{1,0:T(8,128)S(1)} %get-tuple-element.28) | copy-start | bytes 21233668
  62.5 33.8 %collective-permute-start.2 = (f32[768]{0:T(1024)}, f32[768]{0:T(1024)}, u32[]{:S(2)}, u32[]{:S(2)}) collective-permute-start(f32[768]{0:T(1024)} %get-tuple-element.26), channel_id=1, source_target_pairs={{0,1},{1,2},{2,3},{3,4},{4,5},{5,6},{6,7},{7,8},{8,9},{9,10},{10,1... | collective-permute-start | bytes 9224 | tf_op jit(solution)/shard_map/ppermute | solution.py:14
  62.5 33.8 %collective-permute-start.3 = (f32[768]{0:T(1024)}, f32[768]{0:T(1024)}, u32[]{:S(2)}, u32[]{:S(2)}) collective-permute-start(f32[768]{0:T(1024)} %get-tuple-element.27), channel_id=1, source_target_pairs={{1,0},{2,1},{3,2},{4,3},{5,4},{6,5},{7,6},{8,7},{9,8},{10,9},{11,1... | collective-permute-start | bytes 9224 | tf_op jit(solution)/shard_map/ppermute | solution.py:15
  75.1 23.4 %collective-permute-start.4 = (f32[768]{0:T(1024)}, f32[768]{0:T(1024)}, u32[]{:S(2)}, u32[]{:S(2)}) collective-permute-start(f32[768]{0:T(1024)} %get-tuple-element.23), channel_id=1, source_target_pairs={{0,1},{1,2},{2,3},{3,4},{4,5},{5,6},{6,7},{7,8},{8,9},{9,10},{10,1... | collective-permute-start | bytes 9224 | tf_op jit(solution)/shard_map/ppermute | solution.py:14
  75.1 24.0 %collective-permute-start.5 = (f32[768]{0:T(1024)}, f32[768]{0:T(1024)}, u32[]{:S(2)}, u32[]{:S(2)}) collective-permute-start(f32[768]{0:T(1024)} %get-tuple-element.24), channel_id=1, source_target_pairs={{1,0},{2,1},{3,2},{4,3},{5,4},{6,5},{7,6},{8,7},{9,8},{10,9},{11,1... | collective-permute-start | bytes 9224 | tf_op jit(solution)/shard_map/ppermute | solution.py:15
  101.8 1.3 collective-permute-start.7
  101.8 8.2 %collective-permute-start.6 = (f32[768]{0:T(1024)S(1)}, f32[768]{0:T(1024)S(1)}, u32[]{:S(2)}, u32[]{:S(2)}) collective-permute-start(f32[768]{0:T(1024)S(1)} %get-tuple-element.18), channel_id=1, source_target_pairs={{0,1},{1,2},{2,3},{3,4},{4,5},{5,6},{6,7},{7,8},{8,9},{9,10},{10,1... | collective-permute-start | bytes 9224 | tf_op jit(solution)/shard_map/ppermute | solution.py:14
  122.6 84.3 %collective-permute-start.8 = (f32[768,1152]{0,1:T(8,128)}, f32[768,1152]{0,1:T(8,128)S(1)}, u32[]{:S(2)}, u32[]{:S(2)}) collective-permute-start(f32[768,1152]{0,1:T(8,128)} %get-tuple-element.19), channel_id=1, source_target_pairs={{0,1},{1,2},{2,3},{3,4},{4,5},{5,6},{6,7},{7,8},{8,9},{9,10},{10,1... | collective-permute-start | bytes 10616840 | tf_op jit(solution)/shard_map/ppermute | solution.py:14
  122.6 84.3 %collective-permute-start.9 = (f32[768,1152]{0,1:T(8,128)}, f32[768,1152]{0,1:T(8,128)}, u32[]{:S(2)}, u32[]{:S(2)}) collective-permute-start(f32[768,1152]{0,1:T(8,128)} %get-tuple-element.20), channel_id=1, source_target_pairs={{1,0},{2,1},{3,2},{4,3},{5,4},{6,5},{7,6},{8,7},{9,8},{10,9},{11,1... | collective-permute-start | bytes 10616840 | tf_op jit(solution)/shard_map/ppermute | solution.py:15
where the time goes:
time: 221 us; the launch traced here: 220 us
  waiting for transfers between devices  112 us (51%)
  local copies, waits for them, and re-layouts  31.6 us (14%)
  starting transfers between devices  28.7 us (13%)
  matrix products  27.3 us (12%)
  other arithmetic  18.9 us (9%)
    ppermute x5, waiting for transfers between devices, padded(): before = lax.ppermute(last, axis, up)  75.1 us
    ppermute x5, waiting for transfers between devices, padded(): after = lax.ppermute(first, axis, down)  36.7 us
    ppermute x5, starting transfers between devices, padded(): after = lax.ppermute(first, axis, down)  28.1 us
    gather x1, local copies, waits for them, and re-layouts, body(): positive = jnp.diagonal(scores[:, height:2 * height])  14.4 us
    dot_general x1, matrix products, body(): jnp.dot(weights, cap_window, preferred_element_type=jnp.float32)  13 us
    dot_general x1, matrix products, body(): lax.dot_general(weights, img_half, (((0,), (0,)), ((), ())), preferred_el...  9.32 us
    unnamed x14, local copies, waits for them, and re-layouts  7.8 us
    dot_general x1, matrix products, body(): lax.dot_general(img_half, cap_window, (((1,), (1,)), ((), ())), preferred...  4.99 us
  transfers between devices with their start and end apart: 10, of which 5 were waited for; matrix products, arithmetic and copies ran while one was open for 19% of the time, Pallas kernels for 0%

commit v1 on v0

v1 whole, which is shorter than its diff:
```python
import functools

import jax
import jax.numpy as jnp
from jax import lax
from jax.experimental import pallas as pl
from jax.experimental.pallas import tpu as pltpu
from jax.sharding import PartitionSpec as P

TILE = 256
LANES = 128
MIB = 1024 * 1024
F32, BF16 = jnp.float32, jnp.bfloat16
VMEM = pl.BlockSpec(memory_space=pltpu.VMEM)
SMEM = pl.BlockSpec(memory_space=pltpu.SMEM)
HBM = pl.BlockSpec(memory_space=pltpu.HBM)
PARTS = ((0, 256), (256, 256), (512, 256))


def array(dtype, *shape):
    return jax.ShapeDtypeStruct(shape, dtype)


def in_hbm(dtype, *shape):
    return pltpu.HBM(shape, dtype)


def call(kernel, ins, outs, shapes, name, macs=0, scratch=(), limit=6):
    def run(*operands):
        return inner(
            *(
                pltpu.with_memory_space_constraint(value, pltpu.HBM) if spec is HBM else value
                for value, spec in zip(operands, ins, strict=True)
            )
        )

    inner = pl.pallas_call(
        kernel,
        in_specs=ins,
        out_specs=outs,
        out_shape=shapes,
        scratch_shapes=list(scratch),
        compiler_params=pltpu.CompilerParams(vmem_limit_bytes=limit * MIB),
        cost_estimate=pl.CostEstimate(
            flops=2 * macs, bytes_accessed=2_000_000, transcendentals=0
        ),
        name=name,
    )
    return run


def tiles(height):
    return [slice(start, min(start + TILE, height)) for start in range(0, height, TILE)]


def dot_nt(a, b):
    return lax.dot_general(a, b, (((1,), (1,)), ((), ())), preferred_element_type=F32)


def to_lanes(column):
    return jnp.transpose(jnp.broadcast_to(column, (column.shape[0], LANES)))[0:1, :]


def to_rows(lanes, width):
    block = jnp.transpose(jnp.broadcast_to(lanes, (LANES, lanes.shape[1])))
    copies = -(-width // LANES)
    return jnp.concatenate([block] * copies, axis=1)[:, :width]


def unit_rows(raw):
    wide = raw.astype(F32)
    inverse = lax.rsqrt(jnp.sum(wide * wide, axis=-1, keepdims=True) + 1e-06)
    return wide * inverse, inverse


def diagonal(shape, start):
    here = lax.broadcasted_iota(jnp.int32, shape, 0) + start
    return here == lax.broadcasted_iota(jnp.int32, shape, 1)


def weigh(scores, own_lse, other_lse, start=None):
    weights = 0.5 * jnp.exp(scores - own_lse) + 0.5 * jnp.exp(scores - other_lse)
    if start is not None:
        weights = weights - diagonal(scores.shape, start).astype(F32)
    return weights.astype(BF16)


def project(raw, grad):
    unit, inverse = unit_rows(raw)
    return inverse * (grad - unit * jnp.sum(unit * grad, axis=-1, keepdims=True))


def normalize(*arrays):
    height, width = arrays[0].shape
    count = len(arrays)

    def kernel(*refs):
        for src, dst in zip(refs[:count], refs[count:]):
            for rows in tiles(height):
                dst[rows, :] = unit_rows(src[rows, :])[0].astype(BF16)

    return call(
        kernel, [VMEM] * count, [VMEM] * count, [array(BF16, height, width)] * count, "unit_rows"
    )(*arrays)


def start_copy(source, target, sem):
    copy = pltpu.make_async_copy(source, target, sem)
    copy.start()
    return copy


def start_copy(source, target, sem):
    copy = pltpu.make_async_copy(source, target, sem)
    copy.start()
    return copy


def near_scores(scale, img, cap, mate_img, mate_cap):
    height, width = img.shape

    def kernel(scale_ref, img_ref, cap_ref, mate_img_ref, mate_cap_ref, *outs):
        factor = scale_ref[0]
        for own_ref, opp_ref, mate_ref, (first_ref, second_ref, stats_ref) in (
            (img_ref, cap_ref, mate_cap_ref, outs[:3]),
            (cap_ref, img_ref, mate_img_ref, outs[3:]),
        ):
            for rows in tiles(height):
                first = factor * dot_nt(own_ref[rows, :], opp_ref[...])
                second = factor * dot_nt(own_ref[rows, :], mate_ref[...])
                first_ref[rows, :] = first
                second_ref[rows, :] = second
                peak = jnp.maximum(
                    jnp.max(first, axis=1, keepdims=True), jnp.max(second, axis=1, keepdims=True)
                )
                total = jnp.sum(jnp.exp(first - peak), axis=1, keepdims=True) + jnp.sum(
                    jnp.exp(second - peak), axis=1, keepdims=True
                )
                diag = jnp.where(diagonal(first.shape, rows.start), first, 0.0)
                stats_ref[0:1, rows] = to_lanes(peak)
                stats_ref[1:2, rows] = to_lanes(total)
                stats_ref[2:3, rows] = to_lanes(jnp.sum(diag, axis=1, keepdims=True))

    square, stats = array(F32, height, height), array(F32, 8, height)
    return call(
        kernel,
        [SMEM] + [VMEM] * 4,
        [VMEM] * 6,
        [square, square, stats] * 2,
        "near_scores",
        4 * height * height * width,
    )(scale, img, cap, mate_img, mate_cap)


def far_scores(scale, own, far, stats):
    height, width = own.shape

    def kernel(scale_ref, own_ref, far_ref, stats_ref, scores_ref, half_ref, msg_ref):
        factor = scale_ref[0]
        for rows in tiles(height):
            half_ref[rows, :] = unit_rows(far_ref[rows, :])[0].astype(BF16)
        tops, sums = [], []
        for rows in tiles(height):
            scores = factor * dot_nt(own_ref[rows, :], half_ref[...])
            scores_ref[rows, :] = scores
            peak = jnp.max(scores, axis=1, keepdims=True)
            total = jnp.sum(jnp.exp(scores - peak), axis=1, keepdims=True)
            peak, total = to_lanes(peak), to_lanes(total)
            before = stats_ref[0:1, rows]
            top = jnp.maximum(before, peak)
            summed = stats_ref[1:2, rows] * jnp.exp(before - top) + total * jnp.exp(peak - top)
            msg_ref[0:1, rows] = top + jnp.log(summed)
            tops.append(jnp.max(scores, axis=0, keepdims=True))
            sums.append(jnp.sum(jnp.exp(scores - tops[-1]), axis=0, keepdims=True))
        col_top = functools.reduce(jnp.maximum, tops)
        msg_ref[1:2, :] = col_top
        msg_ref[2:3, :] = sum(s * jnp.exp(t - col_top) for s, t in zip(sums, tops))

    return call(
        kernel,
        [SMEM] + [VMEM] * 3,
        [VMEM] * 3,
        [array(F32, height, height), array(BF16, height, width), array(F32, 8, height)],
        "far_scores",
        height * height * width,
    )(scale, own, far, stats)


def finish_columns(col_stats, far_message, message, row_stats):
    height = col_stats.shape[1]

    def kernel(stats_ref, far_ref, msg_ref, row_ref, out_ref, loss_ref):
        before, far_top = stats_ref[0:1, :], far_ref[1:2, :]
        top = jnp.maximum(before, far_top)
        summed = stats_ref[1:2, :] * jnp.exp(before - top) + far_ref[2:3, :] * jnp.exp(
            far_top - top
        )
        lse = top + jnp.log(summed)
        out_ref[0:1, :] = lse
        positive = row_ref[2:3, :]
        loss = 0.5 * (msg_ref[0:1, :] - positive) + 0.5 * (lse - positive)
        loss_ref[...] = loss.reshape(height)

    return call(
        kernel,
        [VMEM] * 4,
        [VMEM] * 2,
        [array(F32, 8, height), array(F32, height)],
        "finish_columns",
    )(col_stats, far_message, message, row_stats)


def caption_gradient(scale, scores, own, own_message, messages, others, part, far_message):
    height, width = own.shape
    count, (start, length) = len(others), PARTS[0]

    def kernel(scale_ref, own_ref, own_msg_ref, part_ref, far_msg_ref, *refs):
        score_refs, msg_refs, other_refs = (refs[i * count : (i + 1) * count] for i in range(3))
        factor = scale_ref[0]
        other = unit_rows(part_ref[...])[0].astype(BF16)
        for rows in tiles(height):
            weights = weigh(
                factor * dot_nt(own_ref[rows, :], other),
                to_rows(own_msg_ref[0:1, rows], length),
                far_msg_ref[0:1, start : start + length],
            )
            total = jnp.dot(weights, other, preferred_element_type=F32)
            own_lse = to_rows(own_msg_ref[0:1, rows], height)
            for k in range(count):
                weights = weigh(
                    score_refs[k][rows, :],
                    own_lse,
                    msg_refs[k][0:1, :],
                    rows.start if k == 0 else None,
                )
                total += jnp.dot(weights, other_refs[k][...], preferred_element_type=F32)
            refs[-1][rows, :] = total

    return call(
        kernel,
        [SMEM] + [VMEM] * (4 + 3 * count),
        VMEM,
        array(F32, height, width),
        "caption_gradient",
        count * height * height * width + 2 * length * height * width,
    )(scale, own, own_message, part, far_message, *scores, *messages, *others)


def image_gradient(scale, scores, own_message, messages, others, raw):
    height, width = raw.shape
    rows_of = tiles(height)
    count = len(others)

    def kernel(scale_ref, own_ref, *refs):
        score_refs, msg_refs, other_refs = (refs[i * count : (i + 1) * count] for i in range(3))
        raw_ref, out_ref, stage, sems = refs[3 * count :]
        factor = scale_ref[0]
        copies = []
        for index, rows in enumerate(rows_of):
            own_lse = to_rows(own_ref[0:1, rows], height)
            total = None
            for k in range(count):
                weights = weigh(
                    score_refs[k][rows, :],
                    own_lse,
                    msg_refs[k][0:1, :],
                    rows.start if k == 0 else None,
                )
                term = jnp.dot(weights, other_refs[k][...], preferred_element_type=F32)
                total = term if total is None else total + term
            stage[rows, :] = project(raw_ref[rows, :], factor * total)
            copies.append(start_copy(stage.at[rows, :], out_ref.at[rows, :], sems.at[index]))
        for copy in copies:
            copy.wait()

    return call(
        kernel,
        [SMEM] + [VMEM] * (2 + 3 * count),
        HBM,
        in_hbm(F32, height, width),
        "image_gradient",
        count * height * height * width,
        [pltpu.VMEM((height, width), F32), pltpu.SemaphoreType.DMA((len(rows_of),))],
        limit=12,
    )(scale, own_message, *scores, *messages, *others, raw)


def part_gradient(scale, own, own_message, part, message, start, total, raw=None):
    height, width = own.shape
    rows_of = tiles(height)
    count = part.shape[0]
    final = raw is not None

    def kernel(scale_ref, own_ref, own_msg_ref, part_ref, msg_ref, total_ref, *refs):
        factor = scale_ref[0]
        copies = []
        other = unit_rows(part_ref[...])[0].astype(BF16)
        for index, rows in enumerate(rows_of):
            weights = weigh(
                factor * dot_nt(own_ref[rows, :], other),
                to_rows(own_msg_ref[0:1, rows], count),
                msg_ref[0:1, start : start + count],
            )
            total = total_ref[rows, :] + jnp.dot(weights, other, preferred_element_type=F32)
            if final:
                raw_ref, out_ref, stage, sems = refs
                stage[rows, :] = project(raw_ref[rows, :], factor * total)
                copies.append(start_copy(stage.at[rows, :], out_ref.at[rows, :], sems.at[index]))
            else:
                refs[0][rows, :] = total
        for copy in copies:
            copy.wait()

    return call(
        kernel,
        [SMEM] + [VMEM] * (6 if final else 5),
        HBM if final else VMEM,
        (in_hbm if final else array)(F32, height, width),
        "last_part_gradient" if final else "part_gradient",
        2 * count * height * width,
        [pltpu.VMEM((height, width), F32), pltpu.SemaphoreType.DMA((len(rows_of),))]
        if final
        else [],
        limit=12 if final else 6,
    )(scale, own, own_message, part, message, total, *([raw] if final else []))


def body(mate_pairs, far_pairs, images, captions, logit_scale):
    axes = ("gx", "gy")
    to_mate = functools.partial(lax.ppermute, axis_name=axes, perm=mate_pairs)
    to_far = functools.partial(lax.ppermute, axis_name=axes, perm=far_pairs)

    def after(value, cause):
        return lax.optimization_barrier((value, cause))[0]

    def part_of(index):
        start, count = PARTS[index]
        return lax.slice_in_dim(images, start, start + count, axis=0)

    far_raw = to_far(captions)
    parts = [to_far(part_of(0))]
    mate_raw = (to_mate(images), to_mate(captions))

    img, cap = normalize(images, captions)
    mate_img, mate_cap = normalize(*mate_raw)
    img_cap, img_mate, row_stats, cap_img, cap_mate, col_stats = near_scores(
        logit_scale, img, cap, mate_img, mate_cap
    )
    img_far, far_cap, message = far_scores(logit_scale, img, far_raw, row_stats)
    far_message = to_far(message)
    mate_message = to_mate(message)
    parts.append(to_far(after(part_of(1), message)))

    col_message, losses = finish_columns(col_stats, far_message, message, row_stats)
    far_col = to_far(col_message)
    mate_col = to_mate(col_message)
    for index in range(2, len(PARTS)):
        parts.append(to_far(after(part_of(index), col_message)))

    total = caption_gradient(
        logit_scale,
        (cap_img, cap_mate),
        cap,
        col_message,
        (message, mate_message),
        (img, mate_img),
        parts[0],
        far_message,
    )
    grad_images = image_gradient(
        logit_scale,
        (img_cap, img_mate, img_far),
        message,
        (col_message, mate_col, far_col),
        (cap, mate_cap, far_cap),
        images,
    )
    total, grad_images = lax.optimization_barrier((total, grad_images))
    for index, part in enumerate(parts):
        if index == 0:
            continue
        total = part_gradient(
            logit_scale,
            cap,
            col_message,
            part,
            far_message,
            PARTS[index][0],
            total,
            captions if index == len(parts) - 1 else None,
        )
    return losses, grad_images, total


def solution(mesh):
    devices = mesh.size
    mate_pairs = [(i, i ^ 1) for i in range(devices)]
    far_pairs = [(i, (i + 2 * (i % 2) - 1) % devices) for i in range(devices)]
    return jax.shard_map(
        functools.partial(body, mate_pairs, far_pairs),
        mesh=mesh,
        in_specs=(P(("gx", "gy"), None), P(("gx", "gy"), None), P()),
        out_specs=(P(("gx", "gy")), P(("gx", "gy"), None), P(("gx", "gy"), None)),
        check_vma=False,
    )
```

time: 221 us -> 98.3 us (0.44)
  the two profiles are of different devices: /device:TPU:56 before, /device:TPU:0 now
where the time goes in v1:
time: 98.3 us; the launch traced here: 98.2 us
  waiting for transfers between devices  40.9 us (42%)
  Pallas kernels  30 us (31%)
  starting transfers between devices  24.1 us (25%)
  between operations  1.58 us (2%)
  local copies, waits for them, and re-layouts  1.56 us (2%)
    pallas_call x9, Pallas kernels, run(): inner(*(pltpu.with_memory_space_constraint(value, pltpu.HBM) if spec is H...  30 us
    ppermute x1, waiting for transfers between devices, body(): far_raw = to_far(captions)  28.4 us
    ppermute x1, waiting for transfers between devices, body(): far_col = to_far(col_message)  9.93 us
    ppermute x1, starting transfers between devices, body(): far_raw = to_far(captions)  8.47 us
    ppermute x1, starting transfers between devices, body(): far_message = to_far(message)  7.25 us
    ppermute x1, starting transfers between devices, body(): far_col = to_far(col_message)  6.42 us
    ppermute x1, waiting for transfers between devices, body(): far_message = to_far(message)  2.57 us
  transfers between devices with their start and end apart: 10, of which 3 were waited for; matrix products, arithmetic and copies ran while one was open for 2% of the time, Pallas kernels for 26%

profile of v1, /device:TPU:0, one launch (start us, length us, event | category | flops | bytes accessed | tf_op | source)
XLA Modules:
  0.0 98.2 jit_solution(11335229207379450978)
XLA Ops:
  0.6 0.1 collective-permute-start
  0.7 0.5 collective-permute-start.1
  1.2 8.5 %collective-permute-start.2 = (bf16[768,1152]{1,0:T(8,128)(2,1)}, bf16[768,1152]{1,0:T(8,128)(2,1)S(1)}, u32[]{:S(2)}, u32[]{:S(2)}) collective-permute-start(bf16[768,1152]{1,0:T(8,128)(2,1)} %refs_0_.3), channel_id=1, source_target_pairs={{0,255},{1,2},{2,1},{3,4},{4,3},{5,6},{6,5},{7,8},{8,7},{9,10},{10... | collective-permute-start | bytes 5308424 | tf_op jit(solution)/shard_map/ppermute | solution.py:340
  9.7 1.6 %fusion = (bf16[256,1152]{1,0:T(8,128)(2,1)S(1)}, bf16[256,1152]{1,0:T(8,128)(2,1)S(1)}, bf16[256,1152]{1,0:T(8,128)(2,1)S(1)}) fusion(bf16[768,1152]{1,0:T(8,128)(2,1)} %refs_9_.1), kind=kLoop, calls=%fused_computation | loop fusion | bytes 3538944 | tf_op jit(solution)/shard_map/slice | solution.py:338
  11.3 0.4 collective-permute-start.4
  11.7 1.1 %unit_rows.2 = (bf16[768,1152]{1,0:T(8,128)(2,1)S(1)}, bf16[768,1152]{1,0:T(8,128)(2,1)S(1)}) custom-call(bf16[768,1152]{1,0:T(8,128)(2,1)S(1)} %copy-done, bf16[768,1152]{1,0:T(8,128)(2,1)S(1)} %copy-done.1), custom_call_target="tpu_custom_call" | custom-call | bytes 2000000 | tf_op jit(solution)/shard_map/unit_rows/pallas_call | solution.py:30
  13.5 0.0 collective-permute-done.refs_0_
  13.5 1.1 %unit_rows.3 = (bf16[768,1152]{1,0:T(8,128)(2,1)S(1)}, bf16[768,1152]{1,0:T(8,128)(2,1)S(1)}) custom-call(bf16[768,1152]{1,0:T(8,128)(2,1)S(1)} %collective-permute-done.refs_0_, bf16[768,1152]{1,0:T(8,128)(2,1)S(1)} %collective-permute-done.1.refs_1_), custom_call_target="tpu_custom_call" | custom-call | bytes 2000000 | tf_op jit(solution)/shard_map/unit_rows/pallas_call | solution.py:30
  14.6 6.7 %near_scores.1 = (f32[768,768]{1,0:T(8,128)S(1)}, f32[768,768]{1,0:T(8,128)S(1)}, f32[8,768]{1,0:T(8,128)S(1)}, f32[768,768]{1,0:T(8,128)S(1)}, f32[768,768]{1,0:T(8,128)S(1)}, /*index=5*/f32[8,768]{1,0:T(8,128)S(1)}) custom-call(f32[1]{0:T(128)S(6)} %copy.6.scale_ref, bf16[768,1152]{1,0:T(8,128)(2,1)S(1)} %get-tuple-element.22.img_ref.own_ref.refs_4_, ...), custom_call_target="tpu_custom_call" | custom-call | flops 5435817984 | bytes 2000000 | tf_op jit(solution)/shard_map/near_scores/pallas_call | solution.py:30
  21.3 28.4 %collective-permute-done.2.far_ref = bf16[768,1152]{1,0:T(8,128)(2,1)S(1)} collective-permute-done((bf16[768,1152]{1,0:T(8,128)(2,1)}, bf16[768,1152]{1,0:T(8,128)(2,1)S(1)}, u32[]{:S(2)}, u32[]{:S(2)}) %collective-permute-start.2) | collective-permute-done | bytes 1769504 | tf_op jit(solution)/shard_map/ppermute | solution.py:340
  49.7 2.6 %far_scores.1 = (f32[768,768]{1,0:T(8,128)S(1)}, bf16[768,1152]{1,0:T(8,128)(2,1)S(1)}, f32[8,768]{1,0:T(8,128)S(1)}) custom-call(f32[1]{0:T(128)S(6)} %copy.6.scale_ref, bf16[768,1152]{1,0:T(8,128)(2,1)S(1)} %get-tuple-element.22.img_ref.own_ref.refs_4_, bf16[768,1152]{1,0:T(8,128)(2,1)S(1)} %collective-permute-done.2.far_ref, ...), custom_call_target="tpu_custom_call" | custom-call | flops 1358954496 | bytes 2000000 | tf_op jit(solution)/shard_map/far_scores/pallas_call | solution.py:30
  52.2 7.3 %collective-permute-start.3 = (f32[8,768]{1,0:T(8,128)S(1)}, f32[8,768]{1,0:T(8,128)S(1)}, u32[]{:S(2)}, u32[]{:S(2)}) collective-permute-start(f32[8,768]{1,0:T(8,128)S(1)} %get-tuple-element.28.msg_ref.refs_2_.own_ref), channel_id=1, source_target_pairs={{0,255},{1,2},{2,1},{3,4},{4,3},{5,6},{6,5},{7,8},{8,7},{9,10},{10... | collective-permute-start | bytes 73736 | tf_op jit(solution)/shard_map/ppermute | solution.py:350
  59.5 0.2 collective-permute-start.9
  59.7 2.6 %collective-permute-done.3.far_ref.far_msg_ref.msg_ref = f32[8,768]{1,0:T(8,128)S(1)} collective-permute-done((f32[8,768]{1,0:T(8,128)S(1)}, f32[8,768]{1,0:T(8,128)S(1)}, u32[]{:S(2)}, u32[]{:S(2)}) %collective-permute-start.3) | collective-permute-done | bytes 24608 | tf_op jit(solution)/shard_map/ppermute | solution.py:350
  62.3 0.6 finish_columns.1
  62.9 0.0 collective-permute-start.6
  62.9 6.4 %collective-permute-start.7 = (f32[8,768]{1,0:T(8,128)S(1)}, f32[8,768]{1,0:T(8,128)S(1)}, u32[]{:S(2)}, u32[]{:S(2)}) collective-permute-start(f32[8,768]{1,0:T(8,128)S(1)} %get-tuple-element.30.own_msg_ref.refs_3_), channel_id=1, source_target_pairs={{0,255},{1,2},{2,1},{3,4},{4,3},{5,6},{6,5},{7,8},{8,7},{9,10},{10... | collective-permute-start | bytes 73736 | tf_op jit(solution)/shard_map/ppermute | solution.py:355
  69.3 0.0 collective-permute-done.4.part_ref
  69.3 0.8 collective-permute-start.8
  70.0 4.6 %caption_gradient.1.total_ref = f32[768,1152]{1,0:T(8,128)S(1)} custom-call(f32[1]{0:T(128)S(6)} %copy.6.scale_ref, bf16[768,1152]{1,0:T(8,128)(2,1)S(1)} %get-tuple-element.23.cap_ref.own_ref.refs_6_, f32[8,768]{1,0:T(8,128)S(1)} %get-tuple-element.30.own_msg_ref.refs_3_, bf16[256,1152]{1,0:T(8,128)(2,1)S(1)} %collective-permute-done.4.part_ref, ...), custom_call_target="tpu_custom_call" | custom-call | flops 3623878656 | bytes 2000000 | tf_op jit(solution)/shard_map/caption_gradient/pallas_call | solution.py:30
  74.7 9.9 %collective-permute-done.7.refs_5_ = f32[8,768]{1,0:T(8,128)S(1)} collective-permute-done((f32[8,768]{1,0:T(8,128)S(1)}, f32[8,768]{1,0:T(8,128)S(1)}, u32[]{:S(2)}, u32[]{:S(2)}) %collective-permute-start.7) | collective-permute-done | bytes 24608 | tf_op jit(solution)/shard_map/ppermute | solution.py:355
  84.6 7.0 %image_gradient.1 = f32[768,1152]{1,0:T(8,128)} custom-call(f32[1]{0:T(128)S(6)} %copy.6.scale_ref, f32[8,768]{1,0:T(8,128)S(1)} %get-tuple-element.28.msg_ref.refs_2_.own_ref, f32[768,768]{1,0:T(8,128)S(1)} %get-tuple-element.33.refs_0_, f32[768,768]{1,0:T(8,128)S(1)} %get-tuple-element.34.refs_1_, f32[768,768]{1,0:T(8,128)S(1)} %get-tuple-element.35.refs_2_, ...), custom_call_target="tpu_custom_call" | custom-call | flops 4076863488 | bytes 2000000 | tf_op jit(solution)/shard_map/image_gradient/pallas_call | solution.py:30
  91.6 2.2 %part_gradient.1.total_ref = f32[768,1152]{1,0:T(8,128)S(1)} custom-call(f32[1]{0:T(128)S(6)} %copy.6.scale_ref, bf16[768,1152]{1,0:T(8,128)(2,1)S(1)} %get-tuple-element.23.cap_ref.own_ref.refs_6_, f32[8,768]{1,0:T(8,128)S(1)} %get-tuple-element.30.own_msg_ref.refs_3_, bf16[256,1152]{1,0:T(8,128)(2,1)S(1)} %collective-permute-done.9.part_ref, ...), custom_call_target="tpu_custom_call" | custom-call | flops 905969664 | bytes 2000000 | tf_op jit(solution)/shard_map/part_gradient/pallas_call | solution.py:30
  93.8 4.2 %last_part_gradient.1 = f32[768,1152]{1,0:T(8,128)} custom-call(f32[1]{0:T(128)S(6)} %copy.6.scale_ref, bf16[768,1152]{1,0:T(8,128)(2,1)S(1)} %get-tuple-element.23.cap_ref.own_ref.refs_6_, f32[8,768]{1,0:T(8,128)S(1)} %get-tuple-element.30.own_msg_ref.refs_3_, bf16[256,1152]{1,0:T(8,128)(2,1)S(1)} %collective-permute-done.8.part_ref, ...), custom_call_target="tpu_custom_call" | custom-call | flops 905969664 | bytes 2000000 | tf_op jit(solution)/shard_map/last_part_gradient/pallas_call | solution.py:30
  (10 shorter events, 0.0 us)
Async XLA Ops:
  0.6 11.1 %copy-start = (bf16[768,1152]{1,0:T(8,128)(2,1)S(1)}, bf16[768,1152]{1,0:T(8,128)(2,1)}, u32[]{:S(2)}) copy-start(bf16[768,1152]{1,0:T(8,128)(2,1)} %refs_9_.1) | copy-start | bytes 5308420
  0.6 11.1 %copy-start.1 = (bf16[768,1152]{1,0:T(8,128)(2,1)S(1)}, bf16[768,1152]{1,0:T(8,128)(2,1)}, u32[]{:S(2)}) copy-start(bf16[768,1152]{1,0:T(8,128)(2,1)} %refs_0_.3) | copy-start | bytes 5308420
  0.6 12.8 %collective-permute-start = (bf16[768,1152]{1,0:T(8,128)(2,1)}, bf16[768,1152]{1,0:T(8,128)(2,1)S(1)}, u32[]{:S(2)}, u32[]{:S(2)}) collective-permute-start(bf16[768,1152]{1,0:T(8,128)(2,1)} %refs_9_.1), channel_id=1, source_target_pairs={{0,1},{1,0},{2,3},{3,2},{4,5},{5,4},{6,7},{7,6},{8,9},{9,8},{10,11... | collective-permute-start | bytes 5308424 | tf_op jit(solution)/shard_map/ppermute | solution.py:342
  0.7 12.8 %collective-permute-start.1 = (bf16[768,1152]{1,0:T(8,128)(2,1)}, bf16[768,1152]{1,0:T(8,128)(2,1)S(1)}, u32[]{:S(2)}, u32[]{:S(2)}) collective-permute-start(bf16[768,1152]{1,0:T(8,128)(2,1)} %refs_0_.3), channel_id=1, source_target_pairs={{0,1},{1,0},{2,3},{3,2},{4,5},{5,4},{6,7},{7,6},{8,9},{9,8},{10,11... | collective-permute-start | bytes 5308424 | tf_op jit(solution)/shard_map/ppermute | solution.py:342
  1.2 48.4 %collective-permute-start.2 = (bf16[768,1152]{1,0:T(8,128)(2,1)}, bf16[768,1152]{1,0:T(8,128)(2,1)S(1)}, u32[]{:S(2)}, u32[]{:S(2)}) collective-permute-start(bf16[768,1152]{1,0:T(8,128)(2,1)} %refs_0_.3), channel_id=1, source_target_pairs={{0,255},{1,2},{2,1},{3,4},{4,3},{5,6},{6,5},{7,8},{8,7},{9,10},{10... | collective-permute-start | bytes 5308424 | tf_op jit(solution)/shard_map/ppermute | solution.py:340
  11.3 58.0 %collective-permute-start.4 = (bf16[256,1152]{1,0:T(8,128)(2,1)S(1)}, bf16[256,1152]{1,0:T(8,128)(2,1)S(1)}, u32[]{:S(2)}, u32[]{:S(2)}) collective-permute-start(bf16[256,1152]{1,0:T(8,128)(2,1)S(1)} %get-tuple-element.42), channel_id=1, source_target_pairs={{0,255},{1,2},{2,1},{3,4},{4,3},{5,6},{6,5},{7,8},{8,7},{9,10},{10... | collective-permute-start | bytes 1769480 | tf_op jit(solution)/shard_map/ppermute | solution.py:341
  52.2 10.0 %collective-permute-start.3 = (f32[8,768]{1,0:T(8,128)S(1)}, f32[8,768]{1,0:T(8,128)S(1)}, u32[]{:S(2)}, u32[]{:S(2)}) collective-permute-start(f32[8,768]{1,0:T(8,128)S(1)} %get-tuple-element.28.msg_ref.refs_2_.own_ref), channel_id=1, source_target_pairs={{0,255},{1,2},{2,1},{3,4},{4,3},{5,6},{6,5},{7,8},{8,7},{9,10},{10... | collective-permute-start | bytes 73736 | tf_op jit(solution)/shard_map/ppermute | solution.py:350
  59.5 10.6 %collective-permute-start.5 = (f32[8,768]{1,0:T(8,128)S(1)}, f32[8,768]{1,0:T(8,128)S(1)}, u32[]{:S(2)}, u32[]{:S(2)}) collective-permute-start(f32[8,768]{1,0:T(8,128)S(1)} %get-tuple-element.28.msg_ref.refs_2_.own_ref), channel_id=1, source_target_pairs={{0,1},{1,0},{2,3},{3,2},{4,5},{5,4},{6,7},{7,6},{8,9},{9,8},{10,11... | collective-permute-start | bytes 73736 | tf_op jit(solution)/shard_map/ppermute | solution.py:351
  59.5 32.1 %collective-permute-start.9 = (bf16[256,1152]{1,0:T(8,128)(2,1)S(1)}, bf16[256,1152]{1,0:T(8,128)(2,1)S(1)}, u32[]{:S(2)}, u32[]{:S(2)}) collective-permute-start(bf16[256,1152]{1,0:T(8,128)(2,1)S(1)} %get-tuple-element.39), channel_id=1, source_target_pairs={{0,255},{1,2},{2,1},{3,4},{4,3},{5,6},{6,5},{7,8},{8,7},{9,10},{10... | collective-permute-start | bytes 1769480 | tf_op jit(solution)/shard_map/ppermute | solution.py:352
  62.9 11.8 %collective-permute-start.6 = (f32[8,768]{1,0:T(8,128)S(1)}, f32[8,768]{1,0:T(8,128)S(1)}, u32[]{:S(2)}, u32[]{:S(2)}) collective-permute-start(f32[8,768]{1,0:T(8,128)S(1)} %get-tuple-element.30.own_msg_ref.refs_3_), channel_id=1, source_target_pairs={{0,1},{1,0},{2,3},{3,2},{4,5},{5,4},{6,7},{7,6},{8,9},{9,8},{10,11... | collective-permute-start | bytes 73736 | tf_op jit(solution)/shard_map/ppermute | solution.py:356
  62.9 21.7 %collective-permute-start.7 = (f32[8,768]{1,0:T(8,128)S(1)}, f32[8,768]{1,0:T(8,128)S(1)}, u32[]{:S(2)}, u32[]{:S(2)}) collective-permute-start(f32[8,768]{1,0:T(8,128)S(1)} %get-tuple-element.30.own_msg_ref.refs_3_), channel_id=1, source_target_pairs={{0,255},{1,2},{2,1},{3,4},{4,3},{5,6},{6,5},{7,8},{8,7},{9,10},{10... | collective-permute-start | bytes 73736 | tf_op jit(solution)/shard_map/ppermute | solution.py:355
  69.3 24.5 %collective-permute-start.8 = (bf16[256,1152]{1,0:T(8,128)(2,1)S(1)}, bf16[256,1152]{1,0:T(8,128)(2,1)S(1)}, u32[]{:S(2)}, u32[]{:S(2)}) collective-permute-start(bf16[256,1152]{1,0:T(8,128)(2,1)S(1)} %get-tuple-element.38), channel_id=1, source_target_pairs={{0,255},{1,2},{2,1},{3,4},{4,3},{5,6},{6,5},{7,8},{8,7},{9,10},{10... | collective-permute-start | bytes 1769480 | tf_op jit(solution)/shard_map/ppermute | solution.py:358

commit v2 on v1

--- a/solution.py
+++ b/solution.py
@@ -14,7 +14,7 @@
 VMEM = pl.BlockSpec(memory_space=pltpu.VMEM)
 SMEM = pl.BlockSpec(memory_space=pltpu.SMEM)
 HBM = pl.BlockSpec(memory_space=pltpu.HBM)
-PARTS = ((0, 256), (256, 256), (512, 256))
+PARTS = ((0, 320), (320, 256), (576, 192))
 
 
 def array(dtype, *shape):
@@ -71,6 +71,11 @@
     wide = raw.astype(F32)
     inverse = lax.rsqrt(jnp.sum(wide * wide, axis=-1, keepdims=True) + 1e-06)
     return wide * inverse, inverse
+
+
+def joint_lse(peak, total, other_peak, other_total):
+    top = jnp.maximum(peak, other_peak)
+    return top + jnp.log(total * jnp.exp(peak - top) + other_total * jnp.exp(other_peak - top))
 
 
 def diagonal(shape, start):
@@ -152,10 +157,12 @@
     )(scale, img, cap, mate_img, mate_cap)
 
 
-def far_scores(scale, own, far, stats):
+def far_scores(scale, own, far, stats, col_stats):
     height, width = own.shape
 
-    def kernel(scale_ref, own_ref, far_ref, stats_ref, scores_ref, half_ref, msg_ref):
+    def kernel(
+        scale_ref, own_ref, far_ref, stats_ref, col_stats_ref, scores_ref, half_ref, msg_ref
+    ):
         factor = scale_ref[0]
         for rows in tiles(height):
             half_ref[rows, :] = unit_rows(far_ref[rows, :])[0].astype(BF16)
@@ -166,48 +173,48 @@
             peak = jnp.max(scores, axis=1, keepdims=True)
             total = jnp.sum(jnp.exp(scores - peak), axis=1, keepdims=True)
             peak, total = to_lanes(peak), to_lanes(total)
-            before = stats_ref[0:1, rows]
-            top = jnp.maximum(before, peak)
-            summed = stats_ref[1:2, rows] * jnp.exp(before - top) + total * jnp.exp(peak - top)
-            msg_ref[0:1, rows] = top + jnp.log(summed)
+            msg_ref[0:1, rows] = joint_lse(
+                stats_ref[0:1, rows], stats_ref[1:2, rows], peak, total
+            )
             tops.append(jnp.max(scores, axis=0, keepdims=True))
             sums.append(jnp.sum(jnp.exp(scores - tops[-1]), axis=0, keepdims=True))
         col_top = functools.reduce(jnp.maximum, tops)
+        col_sum = sum(s * jnp.exp(t - col_top) for s, t in zip(sums, tops))
         msg_ref[1:2, :] = col_top
-        msg_ref[2:3, :] = sum(s * jnp.exp(t - col_top) for s, t in zip(sums, tops))
-
-    return call(
-        kernel,
-        [SMEM] + [VMEM] * 3,
+        msg_ref[2:3, :] = col_sum
+        msg_ref[3:5, :] = col_stats_ref[0:2, :]
+
+    return call(
+        kernel,
+        [SMEM] + [VMEM] * 4,
         [VMEM] * 3,
         [array(F32, height, height), array(BF16, height, width), array(F32, 8, height)],
         "far_scores",
         height * height * width,
-    )(scale, own, far, stats)
-
-
-def finish_columns(col_stats, far_message, message, row_stats):
-    height = col_stats.shape[1]
-
-    def kernel(stats_ref, far_ref, msg_ref, row_ref, out_ref, loss_ref):
-        before, far_top = stats_ref[0:1, :], far_ref[1:2, :]
-        top = jnp.maximum(before, far_top)
-        summed = stats_ref[1:2, :] * jnp.exp(before - top) + far_ref[2:3, :] * jnp.exp(
-            far_top - top
-        )
-        lse = top + jnp.log(summed)
+    )(scale, own, far, stats, col_stats)
+
+
+def finish_columns(far_message, message, row_stats):
+    height = message.shape[1]
+
+    def kernel(far_ref, msg_ref, row_ref, out_ref, loss_ref):
+        def column_lse(near, far):
+            return joint_lse(near[3:4, :], near[4:5, :], far[1:2, :], far[2:3, :])
+
+        lse = column_lse(msg_ref, far_ref)
         out_ref[0:1, :] = lse
+        out_ref[1:2, :] = column_lse(far_ref, msg_ref)
         positive = row_ref[2:3, :]
         loss = 0.5 * (msg_ref[0:1, :] - positive) + 0.5 * (lse - positive)
         loss_ref[...] = loss.reshape(height)
 
     return call(
         kernel,
-        [VMEM] * 4,
+        [VMEM] * 3,
         [VMEM] * 2,
         [array(F32, 8, height), array(F32, height)],
         "finish_columns",
-    )(col_stats, far_message, message, row_stats)
+    )(far_message, message, row_stats)
 
 
 def caption_gradient(scale, scores, own, own_message, messages, others, part, far_message):
@@ -250,10 +257,11 @@
     height, width = raw.shape
     rows_of = tiles(height)
     count = len(others)
-
-    def kernel(scale_ref, own_ref, *refs):
+    messages, lse_rows = zip(*messages)
+
+    def kernel(scale_ref, own_ref, raw_ref, *refs):
         score_refs, msg_refs, other_refs = (refs[i * count : (i + 1) * count] for i in range(3))
-        raw_ref, out_ref, stage, sems = refs[3 * count :]
+        out_ref, stage, sems = refs[3 * count :]
         factor = scale_ref[0]
         copies = []
         for index, rows in enumerate(rows_of):
@@ -263,7 +271,7 @@
                 weights = weigh(
                     score_refs[k][rows, :],
                     own_lse,
-                    msg_refs[k][0:1, :],
+                    msg_refs[k][lse_rows[k] : lse_rows[k] + 1, :],
                     rows.start if k == 0 else None,
                 )
                 term = jnp.dot(weights, other_refs[k][...], preferred_element_type=F32)
@@ -282,7 +290,7 @@
         count * height * height * width,
         [pltpu.VMEM((height, width), F32), pltpu.SemaphoreType.DMA((len(rows_of),))],
         limit=12,
-    )(scale, own_message, *scores, *messages, *others, raw)
+    )(scale, own_message, raw, *scores, *messages, *others)
 
 
 def part_gradient(scale, own, own_message, part, message, start, total, raw=None):
@@ -346,16 +354,15 @@
     img_cap, img_mate, row_stats, cap_img, cap_mate, col_stats = near_scores(
         logit_scale, img, cap, mate_img, mate_cap
     )
-    img_far, far_cap, message = far_scores(logit_scale, img, far_raw, row_stats)
+
+    img_far, far_cap, message = far_scores(logit_scale, img, far_raw, row_stats, col_stats)
     far_message = to_far(message)
     mate_message = to_mate(message)
-    parts.append(to_far(after(part_of(1), message)))
-
-    col_message, losses = finish_columns(col_stats, far_message, message, row_stats)
-    far_col = to_far(col_message)
+    for index in range(1, len(PARTS)):
+        parts.append(to_far(after(part_of(index), message)))
+
+    col_message, losses = finish_columns(far_message, message, row_stats)
     mate_col = to_mate(col_message)
-    for index in range(2, len(PARTS)):
-        parts.append(to_far(after(part_of(index), col_message)))
 
     total = caption_gradient(
         logit_scale,
@@ -367,27 +374,26 @@
         parts[0],
         far_message,
     )
+    mate_col, total = lax.optimization_barrier((mate_col, total))
     grad_images = image_gradient(
         logit_scale,
-        (img_cap, img_mate, img_far),
+        (img_cap, img_far, img_mate),
         message,
-        (col_message, mate_col, far_col),
-        (cap, mate_cap, far_cap),
+        ((col_message, 0), (col_message, 1), (mate_col, 0)),
+        (cap, far_cap, mate_cap),
         images,
     )
     total, grad_images = lax.optimization_barrier((total, grad_images))
-    for index, part in enumerate(parts):
-        if index == 0:
-            continue
+    for index in range(1, len(PARTS)):
         total = part_gradient(
             logit_scale,
             cap,
             col_message,
-            part,
+            parts[index],
             far_message,
             PARTS[index][0],
             total,
-            captions if index == len(parts) - 1 else None,
+            captions if index == len(PARTS) - 1 else None,
         )
     return losses, grad_images, total
 

time: 98.3 us -> 94.3 us (0.959)
  waiting for transfers between devices: 40.9 us -> 32.5 us
  local copies, waits for them, and re-layouts: 1.56 us -> 4.21 us
  Pallas kernels: 30 us -> 32.2 us
    ppermute x3 -> x2, waiting for transfers between devices: 9.93 us -> 6.57 us  [body(): parts.append(to_far(after(part_of(index), message)))]
    unnamed x4 -> x8, local copies, waits for them, and re-layouts: 0.01 us -> 2.96 us
    ppermute x1, waiting for transfers between devices: 2.57 us -> 0.01 us  [body(): far_message = to_far(message)]
    ppermute x1, waiting for transfers between devices: 28.4 us -> 25.9 us  [body(): far_raw = to_far(captions)]
    pallas_call x9, Pallas kernels: 30 us -> 32.2 us  [run(): inner(*(pltpu.with_memory_space_constraint(value, pltpu.HBM) if spec is H...]
    ppermute x3 -> x2, starting transfers between devices: 7.37 us -> 7.26 us  [body(): parts.append(to_far(after(part_of(index), message)))]
  transfers between devices with their start and end apart: 10 -> 9, of which waited for: 3 -> 2; matrix products, arithmetic and copies ran while one was open for 2% -> 1% of each run, Pallas kernels for 26% -> 30%
where the time goes in v2:
time: 94.3 us; the launch traced here: 94.1 us
  waiting for transfers between devices  32.5 us (34%)
  Pallas kernels  32.2 us (34%)
  starting transfers between devices  23.7 us (25%)
  local copies, waits for them, and re-layouts  4.21 us (4%)
  between operations  1.58 us (2%)
    pallas_call x9, Pallas kernels, run(): inner(*(pltpu.with_memory_space_constraint(value, pltpu.HBM) if spec is H...  32.2 us
    ppermute x1, waiting for transfers between devices, body(): far_raw = to_far(captions)  25.9 us
    ppermute x1, starting transfers between devices, body(): far_raw = to_far(captions)  8.47 us
    ppermute x2, starting transfers between devices, body(): parts.append(to_far(after(part_of(index), message)))  7.26 us
    ppermute x1, starting transfers between devices, body(): far_message = to_far(message)  7.26 us
    ppermute x2, waiting for transfers between devices, body(): parts.append(to_far(after(part_of(index), message)))  6.57 us
    unnamed x8, local copies, waits for them, and re-layouts  2.96 us
  transfers between devices with their start and end apart: 9, of which 2 were waited for; matrix products, arithmetic and copies ran while one was open for 1% of the time, Pallas kernels for 30%

profile of v2, /device:TPU:0, one launch (start us, length us, event | category | flops | bytes accessed | tf_op | source)
XLA Modules:
  0.0 94.1 jit_solution(8481672325439537188)
XLA Ops:
  0.6 0.1 collective-permute-start.1
  0.7 0.5 collective-permute-start.2
  1.2 8.5 %collective-permute-start = (bf16[768,1152]{1,0:T(8,128)(2,1)}, bf16[768,1152]{1,0:T(8,128)(2,1)S(1)}, u32[]{:S(2)}, u32[]{:S(2)}) collective-permute-start(bf16[768,1152]{1,0:T(8,128)(2,1)} %refs_0_.3), channel_id=1, source_target_pairs={{0,255},{1,2},{2,1},{3,4},{4,3},{5,6},{6,5},{7,8},{8,7},{9,10},{10... | collective-permute-start | bytes 5308424 | tf_op jit(solution)/shard_map/ppermute | solution.py:348
  9.7 1.2 %slice.9 = bf16[320,1152]{1,0:T(8,128)(2,1)S(1)} slice(bf16[768,1152]{1,0:T(8,128)(2,1)} %raw_ref.1), slice={[0:320], [0:1152]} | slice | bytes 1474560 | tf_op jit(solution)/shard_map/slice | solution.py:346
  10.9 0.1 collective-permute-start.5
  11.0 0.0 copy-start
  11.0 1.5 %copy-done = bf16[768,1152]{1,0:T(8,128)(2,1)S(1)} copy-done((bf16[768,1152]{1,0:T(8,128)(2,1)S(1)}, bf16[768,1152]{1,0:T(8,128)(2,1)}, u32[]{:S(2)}) %copy-start) | copy-done | bytes 1769496
  12.5 1.5 %copy-done.2 = bf16[768,1152]{1,0:T(8,128)(2,1)S(1)} copy-done((bf16[768,1152]{1,0:T(8,128)(2,1)S(1)}, bf16[768,1152]{1,0:T(8,128)(2,1)}, u32[]{:S(2)}) %copy-start.2) | copy-done | bytes 1769496
  13.9 1.1 %unit_rows.2 = (bf16[768,1152]{1,0:T(8,128)(2,1)S(1)}, bf16[768,1152]{1,0:T(8,128)(2,1)S(1)}) custom-call(bf16[768,1152]{1,0:T(8,128)(2,1)S(1)} %copy-done, bf16[768,1152]{1,0:T(8,128)(2,1)S(1)} %copy-done.2), custom_call_target="tpu_custom_call" | custom-call | bytes 2000000 | tf_op jit(solution)/shard_map/unit_rows/pallas_call | solution.py:30
  15.7 0.0 collective-permute-done.2.refs_1_
  15.7 1.1 %unit_rows.3 = (bf16[768,1152]{1,0:T(8,128)(2,1)S(1)}, bf16[768,1152]{1,0:T(8,128)(2,1)S(1)}) custom-call(bf16[768,1152]{1,0:T(8,128)(2,1)S(1)} %collective-permute-done.1.refs_0_, bf16[768,1152]{1,0:T(8,128)(2,1)S(1)} %collective-permute-done.2.refs_1_), custom_call_target="tpu_custom_call" | custom-call | bytes 2000000 | tf_op jit(solution)/shard_map/unit_rows/pallas_call | solution.py:30
  16.8 6.9 %near_scores.1 = (f32[768,768]{1,0:T(8,128)S(1)}, f32[768,768]{1,0:T(8,128)S(1)}, f32[8,768]{1,0:T(8,128)S(1)}, f32[768,768]{1,0:T(8,128)S(1)}, f32[768,768]{1,0:T(8,128)S(1)}, /*index=5*/f32[8,768]{1,0:T(8,128)S(1)}) custom-call(f32[1]{0:T(128)S(6)} %copy.6.scale_ref, bf16[768,1152]{1,0:T(8,128)(2,1)S(1)} %get-tuple-element.24.img_ref.own_ref.refs_4_, ...), custom_call_target="tpu_custom_call" | custom-call | flops 5435817984 | bytes 2000000 | tf_op jit(solution)/shard_map/near_scores/pallas_call | solution.py:30
  23.8 25.9 %collective-permute-done.far_ref = bf16[768,1152]{1,0:T(8,128)(2,1)S(1)} collective-permute-done((bf16[768,1152]{1,0:T(8,128)(2,1)}, bf16[768,1152]{1,0:T(8,128)(2,1)S(1)}, u32[]{:S(2)}, u32[]{:S(2)}) %collective-permute-start) | collective-permute-done | bytes 1769504 | tf_op jit(solution)/shard_map/ppermute | solution.py:348
  49.7 2.8 %far_scores.1 = (f32[768,768]{1,0:T(8,128)S(1)}, bf16[768,1152]{1,0:T(8,128)(2,1)S(1)}, f32[8,768]{1,0:T(8,128)S(1)}) custom-call(f32[1]{0:T(128)S(6)} %copy.6.scale_ref, bf16[768,1152]{1,0:T(8,128)(2,1)S(1)} %get-tuple-element.24.img_ref.own_ref.refs_4_, bf16[768,1152]{1,0:T(8,128)(2,1)S(1)} %collective-permute-done.far_ref, ...), custom_call_target="tpu_custom_call" | custom-call | flops 1358954496 | bytes 2000000 | tf_op jit(solution)/shard_map/far_scores/pallas_call | solution.py:30
  52.4 7.3 %collective-permute-start.3 = (f32[8,768]{1,0:T(8,128)S(1)}, f32[8,768]{1,0:T(8,128)S(1)}, u32[]{:S(2)}, u32[]{:S(2)}) collective-permute-start(f32[8,768]{1,0:T(8,128)S(1)} %get-tuple-element.30.msg_ref.refs_2_.own_ref), channel_id=1, source_target_pairs={{0,255},{1,2},{2,1},{3,4},{4,3},{5,6},{6,5},{7,8},{8,7},{9,10},{10... | collective-permute-start | bytes 73736 | tf_op jit(solution)/shard_map/ppermute | solution.py:359
  59.8 0.2 collective-permute-start.8
  60.0 7.1 %collective-permute-start.7 = (bf16[192,1152]{1,0:T(8,128)(2,1)S(1)}, bf16[192,1152]{1,0:T(8,128)(2,1)S(1)}, u32[]{:S(2)}, u32[]{:S(2)}) collective-permute-start(bf16[192,1152]{1,0:T(8,128)(2,1)S(1)} %slice.10), channel_id=1, source_target_pairs={{0,255},{1,2},{2,1},{3,4},{4,3},{5,6},{6,5},{7,8},{8,7},{9,10},{10... | collective-permute-start | bytes 1327112 | tf_op jit(solution)/shard_map/ppermute | solution.py:362
  67.0 0.6 finish_columns.1
  67.7 6.0 %caption_gradient.1.total_ref = f32[768,1152]{1,0:T(8,128)S(1)} custom-call(f32[1]{0:T(128)S(6)} %copy.6.scale_ref, bf16[768,1152]{1,0:T(8,128)(2,1)S(1)} %get-tuple-element.25.cap_ref.own_ref.refs_6_, f32[8,768]{1,0:T(8,128)S(1)} %get-tuple-element.32.own_msg_ref.refs_3_.refs_4_, bf16[320,1152]{1,0:T(8,128)(2,1)S(1)} %collective-permute-done.5.part_ref, ...), custom_call_target="tpu_custom_call" | custom-call | flops 3850371072 | bytes 2000000 | tf_op jit(solution)/shard_map/caption_gradient/pallas_call | solution.py:30
  73.6 7.4 %image_gradient.1 = f32[768,1152]{1,0:T(8,128)} custom-call(f32[1]{0:T(128)S(6)} %copy.6.scale_ref, f32[8,768]{1,0:T(8,128)S(1)} %get-tuple-element.30.msg_ref.refs_2_.own_ref, bf16[768,1152]{1,0:T(8,128)(2,1)S(1)} %copy-done.1, f32[768,768]{1,0:T(8,128)S(1)} %get-tuple-element.36.refs_0_, f32[768,768]{1,0:T(8,128)S(1)} %get-tuple-element.37.refs_1_, ...), custom_call_target="tpu_custom_call" | custom-call | flops 4076863488 | bytes 2000000 | tf_op jit(solution)/shard_map/image_gradient/pallas_call | solution.py:30
  81.0 0.0 copy-start.3
  81.0 2.4 %part_gradient.1.total_ref = f32[768,1152]{1,0:T(8,128)S(1)} custom-call(f32[1]{0:T(128)S(6)} %copy.6.scale_ref, bf16[768,1152]{1,0:T(8,128)(2,1)S(1)} %get-tuple-element.25.cap_ref.own_ref.refs_6_, f32[8,768]{1,0:T(8,128)S(1)} %get-tuple-element.32.own_msg_ref.refs_3_.refs_4_, bf16[256,1152]{1,0:T(8,128)(2,1)S(1)} %collective-permute-done.8.part_ref, ...), custom_call_target="tpu_custom_call" | custom-call | flops 905969664 | bytes 2000000 | tf_op jit(solution)/shard_map/part_gradient/pallas_call | solution.py:30
  83.5 6.6 %collective-permute-done.7.part_ref = bf16[192,1152]{1,0:T(8,128)(2,1)S(1)} collective-permute-done((bf16[192,1152]{1,0:T(8,128)(2,1)S(1)}, bf16[192,1152]{1,0:T(8,128)(2,1)S(1)}, u32[]{:S(2)}, u32[]{:S(2)}) %collective-permute-start.7) | collective-permute-done | bytes 442400 | tf_op jit(solution)/shard_map/ppermute | solution.py:362
  90.0 3.9 %last_part_gradient.1 = f32[768,1152]{1,0:T(8,128)} custom-call(f32[1]{0:T(128)S(6)} %copy.6.scale_ref, bf16[768,1152]{1,0:T(8,128)(2,1)S(1)} %get-tuple-element.25.cap_ref.own_ref.refs_6_, f32[8,768]{1,0:T(8,128)S(1)} %get-tuple-element.32.own_msg_ref.refs_3_.refs_4_, bf16[192,1152]{1,0:T(8,128)(2,1)S(1)} %collective-permute-done.7.part_ref, ...), custom_call_target="tpu_custom_call" | custom-call | flops 679477248 | bytes 2000000 | tf_op jit(solution)/shard_map/last_part_gradient/pallas_call | solution.py:30
  (14 shorter events, 0.1 us)
Async XLA Ops:
  0.6 15.1 %collective-permute-start.1 = (bf16[768,1152]{1,0:T(8,128)(2,1)}, bf16[768,1152]{1,0:T(8,128)(2,1)S(1)}, u32[]{:S(2)}, u32[]{:S(2)}) collective-permute-start(bf16[768,1152]{1,0:T(8,128)(2,1)} %raw_ref.1), channel_id=1, source_target_pairs={{0,1},{1,0},{2,3},{3,2},{4,5},{5,4},{6,7},{7,6},{8,9},{9,8},{10,11... | collective-permute-start | bytes 5308424 | tf_op jit(solution)/shard_map/ppermute | solution.py:350
  0.7 15.0 %collective-permute-start.2 = (bf16[768,1152]{1,0:T(8,128)(2,1)}, bf16[768,1152]{1,0:T(8,128)(2,1)S(1)}, u32[]{:S(2)}, u32[]{:S(2)}) collective-permute-start(bf16[768,1152]{1,0:T(8,128)(2,1)} %refs_0_.3), channel_id=1, source_target_pairs={{0,1},{1,0},{2,3},{3,2},{4,5},{5,4},{6,7},{7,6},{8,9},{9,8},{10,11... | collective-permute-start | bytes 5308424 | tf_op jit(solution)/shard_map/ppermute | solution.py:350
  1.2 48.4 %collective-permute-start = (bf16[768,1152]{1,0:T(8,128)(2,1)}, bf16[768,1152]{1,0:T(8,128)(2,1)S(1)}, u32[]{:S(2)}, u32[]{:S(2)}) collective-permute-start(bf16[768,1152]{1,0:T(8,128)(2,1)} %refs_0_.3), channel_id=1, source_target_pairs={{0,255},{1,2},{2,1},{3,4},{4,3},{5,6},{6,5},{7,8},{8,7},{9,10},{10... | collective-permute-start | bytes 5308424 | tf_op jit(solution)/shard_map/ppermute | solution.py:348
  10.9 56.8 %collective-permute-start.5 = (bf16[320,1152]{1,0:T(8,128)(2,1)S(1)}, bf16[320,1152]{1,0:T(8,128)(2,1)S(1)}, u32[]{:S(2)}, u32[]{:S(2)}) collective-permute-start(bf16[320,1152]{1,0:T(8,128)(2,1)S(1)} %slice.9), channel_id=1, source_target_pairs={{0,255},{1,2},{2,1},{3,4},{4,3},{5,6},{6,5},{7,8},{8,7},{9,10},{10... | collective-permute-start | bytes 2211848 | tf_op jit(solution)/shard_map/ppermute | solution.py:349
  11.0 1.5 %copy-start = (bf16[768,1152]{1,0:T(8,128)(2,1)S(1)}, bf16[768,1152]{1,0:T(8,128)(2,1)}, u32[]{:S(2)}) copy-start(bf16[768,1152]{1,0:T(8,128)(2,1)} %raw_ref.1) | copy-start | bytes 5308420
  12.5 1.5 %copy-start.2 = (bf16[768,1152]{1,0:T(8,128)(2,1)S(1)}, bf16[768,1152]{1,0:T(8,128)(2,1)}, u32[]{:S(2)}) copy-start(bf16[768,1152]{1,0:T(8,128)(2,1)} %refs_0_.3) | copy-start | bytes 5308420
  49.7 10.0 %copy-start.1 = (bf16[768,1152]{1,0:T(8,128)(2,1)S(1)}, bf16[768,1152]{1,0:T(8,128)(2,1)}, u32[]{:S(2)}) copy-start(bf16[768,1152]{1,0:T(8,128)(2,1)} %raw_ref.1) | copy-start | bytes 5308420
  52.4 14.6 %collective-permute-start.3 = (f32[8,768]{1,0:T(8,128)S(1)}, f32[8,768]{1,0:T(8,128)S(1)}, u32[]{:S(2)}, u32[]{:S(2)}) collective-permute-start(f32[8,768]{1,0:T(8,128)S(1)} %get-tuple-element.30.msg_ref.refs_2_.own_ref), channel_id=1, source_target_pairs={{0,255},{1,2},{2,1},{3,4},{4,3},{5,6},{6,5},{7,8},{8,7},{9,10},{10... | collective-permute-start | bytes 73736 | tf_op jit(solution)/shard_map/ppermute | solution.py:359
  59.7 8.0 %collective-permute-start.6 = (f32[8,768]{1,0:T(8,128)S(1)}, f32[8,768]{1,0:T(8,128)S(1)}, u32[]{:S(2)}, u32[]{:S(2)}) collective-permute-start(f32[8,768]{1,0:T(8,128)S(1)} %get-tuple-element.30.msg_ref.refs_2_.own_ref), channel_id=1, source_target_pairs={{0,1},{1,0},{2,3},{3,2},{4,5},{5,4},{6,7},{7,6},{8,9},{9,8},{10,11... | collective-permute-start | bytes 73736 | tf_op jit(solution)/shard_map/ppermute | solution.py:360
  59.8 21.3 %collective-permute-start.8 = (bf16[256,1152]{1,0:T(8,128)(2,1)S(1)}, bf16[256,1152]{1,0:T(8,128)(2,1)S(1)}, u32[]{:S(2)}, u32[]{:S(2)}) collective-permute-start(bf16[256,1152]{1,0:T(8,128)(2,1)S(1)} %slice.11), channel_id=1, source_target_pairs={{0,255},{1,2},{2,1},{3,4},{4,3},{5,6},{6,5},{7,8},{8,7},{9,10},{10... | collective-permute-start | bytes 1769480 | tf_op jit(solution)/shard_map/ppermute | solution.py:362
  60.0 30.1 %collective-permute-start.7 = (bf16[192,1152]{1,0:T(8,128)(2,1)S(1)}, bf16[192,1152]{1,0:T(8,128)(2,1)S(1)}, u32[]{:S(2)}, u32[]{:S(2)}) collective-permute-start(bf16[192,1152]{1,0:T(8,128)(2,1)S(1)} %slice.10), channel_id=1, source_target_pairs={{0,255},{1,2},{2,1},{3,4},{4,3},{5,6},{6,5},{7,8},{8,7},{9,10},{10... | collective-permute-start | bytes 1327112 | tf_op jit(solution)/shard_map/ppermute | solution.py:362
  67.6 6.0 %collective-permute-start.4 = (f32[8,768]{1,0:T(8,128)S(1)}, f32[8,768]{1,0:T(8,128)S(1)}, u32[]{:S(2)}, u32[]{:S(2)}) collective-permute-start(f32[8,768]{1,0:T(8,128)S(1)} %get-tuple-element.32.own_msg_ref.refs_3_.refs_4_), channel_id=1, source_target_pairs={{0,1},{1,0},{2,3},{3,2},{4,5},{5,4},{6,7},{7,6},{8,9},{9,8},{10,11... | collective-permute-start | bytes 73736 | tf_op jit(solution)/shard_map/ppermute | solution.py:365
  81.0 9.0 %copy-start.3 = (bf16[768,1152]{1,0:T(8,128)(2,1)S(1)}, bf16[768,1152]{1,0:T(8,128)(2,1)}, u32[]{:S(2)}) copy-start(bf16[768,1152]{1,0:T(8,128)(2,1)} %refs_0_.3) | copy-start | bytes 5308420
